TPU v7x, 256 devices: a whole 4x4x8 slice. The times are simulated.
256 devices in a mesh: ctx: 8 (over x, y_lo), ch: 32 (over z, y_hi, core).
Axes of the slice: x: 4, y: 4 (y_hi: 2, y_lo: 2; y = y_hi * 2 + y_lo), z: 8, core: 2. Of those that a mesh axis runs over, the one named last changes fastest.
Arguments:
- out_gate: bfloat16 [4096, 8192], P('ctx', 'ch'), may hold values from -6 to 6
- key_proj: bfloat16 [4096, 8192], P('ctx', 'ch'), may hold values from -6 to 6
- value_proj: bfloat16 [4096, 8192], P('ctx', 'ch'), may hold values from -6 to 6
- filters: float32 [4096, 8192], P('ctx', 'ch'), may hold values from -0.5 to 0.5
- skip_gain: float32 [8192], P('ch'), may hold values from -4 to 4
- out_weight: bfloat16 [8192, 8192], P('ch'), may hold values from -0.125 to 0.125
Outputs:
- projected: bfloat16 [4096, 8192], P('ctx', 'ch')
All inputs are finite; a program needn't handle non-finite values.
Results may differ from a plain program's by a relative error of at most 0.02.
Values may be sent and summed in bfloat16 or wider, within the bound.
A program may use at most 128 MiB of HBM per device.

v0:
```python
import functools

import jax
import jax.numpy as jnp
import numpy as np
from jax import lax
from jax.experimental import pallas as pl
from jax.experimental.pallas import tpu as pltpu
from jax.sharding import PartitionSpec as P

MESH = pl.DeviceIdType.MESH
F32 = jnp.float32
BF16 = jnp.bfloat16

CTX = 8
POS = 512
CHAN = 256
SUB = CHAN // CTX
BLOCK = 256
BLOCKS = 16
PIECE = 128
RING = 8


def dot(a, b):
    return jnp.dot(a, b, preferred_element_type=F32)


def tables():
    theta = np.pi * (2 * np.arange(BLOCK) + 1) / (2 * BLOCK)
    at = np.arange(-BLOCK, BLOCK)[:, None] * theta[None, :]
    forward = np.concatenate((np.cos(at), -np.sin(at)), axis=1)
    back_at = theta[:, None] * np.arange(BLOCK)[None, :]
    backward = np.concatenate((np.cos(back_at), -np.sin(back_at)), axis=0) / BLOCK
    return jnp.asarray(forward, BF16), jnp.asarray(backward, BF16)


def kernel(
    gate,
    key,
    value,
    filt,
    skip,
    w,
    fwd,
    bwd,
    out,
    tsend,
    trecv,
    sbuf,
    hbuf,
    zbuf,
    csend,
    crecv,
    gall,
    wbuf,
    pbuf,
    rsend,
    rrecv,
    t_ss,
    t_rs,
    c_ss,
    c_rs,
    g_ss,
    g_rs,
    own_s,
    wc_ss,
    wc_rs,
    wy_ss,
    wy_rs,
    wx_ss,
    wx_rs,
    r_ss,
    r_rs,
    loc_s,
):
    i = lax.axis_index("ctx")
    j = lax.axis_index("ch")
    x, lo = i // 2, i % 2
    z, q = j // 4, j % 4
    hi, core = q // 2, q % 2

    def remote(src, dst, ss, rs, device):
        return pltpu.make_async_remote_copy(
            src_ref=src, dst_ref=dst, send_sem=ss, recv_sem=rs, device_id=device, device_id_type=MESH
        )

    def w_cols(far, high, cor):
        at = (((z + far) % RING) * 4 + high * 2 + cor) * CHAN
        return w.at[:, pl.ds(pl.multiple_of(at, CHAN), CHAN)]

    barrier = pltpu.get_barrier_semaphore()
    friends = [((i + d) % CTX, j) for d in range(1, CTX)]
    friends += [(i, z * 4 + (q + d) % 4) for d in range(1, 4)]
    friends += [(i, ((z + d) % RING) * 4 + q) for d in (1, RING - 1)]
    friends += [(x * 2 + 1 - lo, z * 4 + (1 - hi) * 2 + c) for c in range(2)]
    for friend in friends:
        pl.semaphore_signal(barrier, inc=1, device_id=friend, device_id_type=MESH)

    own_w = [pltpu.make_async_copy(w_cols(d, hi, core), wbuf.at[d, q], own_s.at[d]) for d in range(RING)]
    for copy in own_w:
        copy.start()

    signal = key[...].astype(F32) * value[...].astype(F32)
    tsend[0] = signal.T.astype(BF16)
    pl.semaphore_wait(barrier, len(friends))

    def spread(t):
        copies = []
        for d in range(1, CTX):
            to = (i + d) % CTX
            rows = pl.ds(pl.multiple_of(to * SUB, SUB), SUB)
            copy = remote(tsend.at[t, rows], trecv.at[t, i], t_ss.at[t, d - 1], t_rs.at[t, d - 1], (to, j))
            copy.start()
            copies.append(copy)
        rows = pl.ds(pl.multiple_of(i * SUB, SUB), SUB)
        mine = pltpu.make_async_copy(tsend.at[t, rows], trecv.at[t, i], loc_s.at[t])
        mine.start()
        return copies, mine

    sig_copies, sig_mine = spread(0)
    tsend[1] = filt[...].T.astype(BF16)
    fil_copies, fil_mine = spread(1)

    fars = [4 - x, (4 + x) * ((x + 3) // 4)]
    wy = []
    for e in range(2):
        for c in range(2):
            copy = remote(
                w_cols(fars[e], 1 - hi, c),
                wbuf.at[fars[e], q],
                wy_ss.at[e, c],
                wy_rs.at[e, core],
                (x * 2 + 1 - lo, z * 4 + (1 - hi) * 2 + c),
            )
            copy.start()
            wy.append(copy)
    wc = []
    for d in range(RING):
        copy = remote(
            w_cols(d, hi, 1 - core), wbuf.at[d, q], wc_ss.at[d], wc_rs.at[d], (i, z * 4 + hi * 2 + 1 - core)
        )
        copy.start()
        wc.append(copy)

    sig_mine.wait()
    for copy in sig_copies:
        copy.wait_recv()
    for h in range(2):
        lhs = trecv[0, :, :, h * BLOCK : (h + 1) * BLOCK].reshape(CTX * SUB, BLOCK)
        sbuf[h] = dot(lhs, fwd[BLOCK:, :])
    fil_mine.wait()
    for copy in fil_copies:
        copy.wait_recv()
    hbuf[1] = dot(trecv[1].reshape(CTX * SUB, POS), fwd[...])
    hbuf[0] = dot(trecv[1, :, :, :BLOCK].reshape(CTX * SUB, BLOCK), fwd[BLOCK:, :])
    hbuf[0, SUB:, :] += dot(trecv[1, : CTX - 1, :, BLOCK:].reshape((CTX - 1) * SUB, BLOCK), fwd[:BLOCK, :])

    @pl.loop(0, (SUB // 8) * (BLOCK // 128))
    def _(t):
        row0 = (t // 2) * 8
        lane_re = pl.multiple_of((t % 2) * 128, 128)
        lane_im = pl.multiple_of(BLOCK + (t % 2) * 128, 128)

        def take(ref, a):
            rows = pl.ds(pl.multiple_of((a // 2) * SUB + row0, 8), 8)
            return ref[a % 2, rows, pl.ds(lane_re, 128)], ref[a % 2, rows, pl.ds(lane_im, 128)]

        for a in range(BLOCKS):
            re = im = None
            for d in range(a + 1):
                sr, si = take(sbuf, a - d)
                hr, hm = take(hbuf, d)
                pr = sr * hr - si * hm
                pm = sr * hm + si * hr
                re = pr if re is None else re + pr
                im = pm if im is None else im + pm
            rows = pl.ds(pl.multiple_of((a // 2) * SUB + row0, 8), 8)
            zbuf[a % 2, rows, pl.ds(lane_re, 128)] = re
            zbuf[a % 2, rows, pl.ds(lane_im, 128)] = im

    for h in range(2):
        csend[:, h * BLOCK : (h + 1) * BLOCK] = dot(zbuf[h].astype(BF16), bwd[...]).astype(BF16)

    mine_rows = pl.ds(pl.multiple_of(i * SUB, SUB), SUB)
    back = []
    for d in range(1, CTX):
        to = (i + d) % CTX
        rows = pl.ds(pl.multiple_of(to * SUB, SUB), SUB)
        copy = remote(csend.at[rows], crecv.at[mine_rows], c_ss.at[d - 1], c_rs.at[d - 1], (to, j))
        copy.start()
        back.append(copy)
    back_mine = pltpu.make_async_copy(csend.at[mine_rows], crecv.at[mine_rows], loc_s.at[2])
    back_mine.start()

    for e in range(2):
        for c in range(2):
            remote(
                w_cols(fars[e], 1 - hi, c),
                wbuf.at[fars[e], (1 - hi) * 2 + c],
                wy_ss.at[e, c],
                wy_rs.at[e, c],
                (x * 2 + 1 - lo, z * 4 + (1 - hi) * 2 + c),
            ).wait_recv()
    wx = []
    for e in range(2):
        for d in (1, 3, 2):
            block = wbuf.at[fars[e], pl.ds((1 - hi) * 2, 2)]
            copy = remote(block, block, wx_ss.at[e, d - 1], wx_rs.at[e, d - 1], (((x + d) % 4) * 2 + lo, j))
            copy.start()
            wx.append(copy)

    back_mine.wait()
    for copy in back:
        copy.wait_recv()
    convolved = crecv[...].astype(F32).T
    signal = key[...].astype(F32) * value[...].astype(F32)
    gall[q] = ((convolved + skip[...] * signal) * gate[...].astype(F32)).astype(BF16)
    gath = []
    for d in range(1, 4):
        copy = remote(gall.at[q], gall.at[q], g_ss.at[d - 1], g_rs.at[d - 1], (i, z * 4 + (q + d) % 4))
        copy.start()
        gath.append(copy)

    for copy in own_w:
        copy.wait()
    for copy in wc:
        copy.wait_recv()
    for copy in wx:
        copy.wait_recv()
    for copy in gath:
        copy.wait_recv()

    def partial(far):
        total = dot(gall[0], wbuf[far, 0])
        for k in range(1, 4):
            total += dot(gall[k], wbuf[far, k])
        return total

    ways = ((0, 1), (1, RING - 1))
    pieces = POS // PIECE
    sums = {}
    first = partial(4)
    for way, near in ways:
        for r in range(way * pieces // 2, (way + 1) * pieces // 2):
            rows = pl.ds(r * PIECE, PIECE)
            rsend[way, 0, rows] = first[r * PIECE : (r + 1) * PIECE].astype(BF16)
    for step in range(4):
        if step:
            for way, _ in ways:
                pbuf[way] = partial(4 - step if way == 0 else 4 + step)
        for r in range(pieces):
            for way, near in ways:
                rows = pl.ds(r * PIECE, PIECE)
                half = way * pieces // 2 <= r < (way + 1) * pieces // 2
                if step == 0 and not half:
                    continue
                if step:
                    total = pbuf[way, rows]
                    if step > 1 or half:
                        sums[way, step - 1, r].wait_recv()
                        total = total + rrecv[way, step - 1, rows].astype(F32)
                    rsend[way, step, rows] = total.astype(BF16)
                copy = remote(
                    rsend.at[way, step, rows],
                    rrecv.at[way, step, rows],
                    r_ss.at[way, step, r],
                    r_rs.at[way, step, r],
                    (i, ((z + near) % RING) * 4 + q),
                )
                copy.start()
                sums[way, step, r] = copy
    pbuf[0] = partial(0)
    for r in range(pieces):
        rows = pl.ds(r * PIECE, PIECE)
        total = pbuf[0, rows]
        for way, _ in ways:
            sums[way, 3, r].wait_recv()
            total = total + rrecv[way, 3, rows].astype(F32)
        out[rows, :] = total.astype(BF16)

    for copy in sig_copies + fil_copies + wy + wc + back + wx + gath + list(sums.values()):
        copy.wait_send()


def body(gate, key, value, filt, skip, w, fwd, bwd):
    vmem = pl.BlockSpec(memory_space=pltpu.VMEM)
    dma = pltpu.SemaphoreType.DMA
    return pl.pallas_call(
        kernel,
        out_shape=jax.ShapeDtypeStruct((POS, CHAN), BF16),
        in_specs=[vmem] * 5 + [pl.BlockSpec(memory_space=pl.ANY)] + [vmem] * 2,
        out_specs=vmem,
        scratch_shapes=[
            pltpu.VMEM((2, CHAN, POS), BF16),
            pltpu.VMEM((2, CTX, SUB, POS), BF16),
            pltpu.VMEM((2, CHAN, 2 * BLOCK), F32),
            pltpu.VMEM((2, CHAN, 2 * BLOCK), F32),
            pltpu.VMEM((2, CHAN, 2 * BLOCK), F32),
            pltpu.VMEM((CHAN, POS), BF16),
            pltpu.VMEM((CHAN, POS), BF16),
            pltpu.VMEM((4, POS, CHAN), BF16),
            pltpu.VMEM((RING, 4, CHAN, CHAN), BF16),
            pltpu.VMEM((2, POS, CHAN), F32),
            pltpu.VMEM((2, 4, POS, CHAN), BF16),
            pltpu.VMEM((2, 4, POS, CHAN), BF16),
            dma((2, CTX - 1)),
            dma((2, CTX - 1)),
            dma((CTX - 1,)),
            dma((CTX - 1,)),
            dma((3,)),
            dma((3,)),
            dma((RING,)),
            dma((RING,)),
            dma((RING,)),
            dma((2, 2)),
            dma((2, 2)),
            dma((2, 3)),
            dma((2, 3)),
            dma((2, 4, POS // PIECE)),
            dma((2, 4, POS // PIECE)),
            dma((3,)),
        ],
        compiler_params=pltpu.CompilerParams(
            collective_id=0, has_side_effects=True, vmem_limit_bytes=40 * 1024 * 1024
        ),
        name="hyena",
    )(gate, key, value, filt, skip.reshape(1, CHAN), w, fwd, bwd)


def solution(mesh):
    mapped = jax.shard_map(
        body,
        mesh=mesh,
        in_specs=(P("ctx", "ch"),) * 4 + (P("ch"), P("ch", None), P(), P()),
        out_specs=P("ctx", "ch"),
        check_vma=False,
    )

    def run(out_gate, key_proj, value_proj, filters, skip_gain, out_weight):
        return mapped(out_gate, key_proj, value_proj, filters, skip_gain, out_weight, *tables())

    return run
```

profile of v0, /device:TPU:1, one launch (start us, length us, event | category | flops | bytes accessed | tf_op | source)
XLA Modules:
  0.0 80.6 jit_solution(15430966395965439734)
XLA Ops:
  0.0 0.0 copy-start
  0.0 2.2 %copy-done = bf16[256,8192]{1,0:T(8,128)(2,1)S(1)} copy-done((bf16[256,8192]{1,0:T(8,128)(2,1)S(1)}, bf16[256,8192]{1,0:T(8,128)(2,1)}, u32[]{:S(2)}) %copy-start) | copy-done | bytes 4194328
  2.2 0.0 copy-start.1
  2.2 1.0 %copy-done.1 = f32[512,256]{1,0:T(8,128)S(1)} copy-done((f32[512,256]{1,0:T(8,128)S(1)}, f32[512,256]{1,0:T(8,128)}, u32[]{:S(2)}) %copy-start.1) | copy-done | bytes 524312
  3.2 0.0 copy-start.2
  3.2 1.0 %copy-done.2 = bf16[512,512]{1,0:T(8,128)(2,1)S(1)} copy-done((bf16[512,512]{1,0:T(8,128)(2,1)S(1)}, bf16[512,512]{1,0:T(8,128)(2,1)}, u32[]{:S(2)}) %copy-start.2) | copy-done | bytes 524312
  4.3 0.0 copy-start.3
  4.3 0.9 %copy-done.3 = bf16[512,256]{1,0:T(8,128)(2,1)S(1)} copy-done((bf16[512,256]{1,0:T(8,128)(2,1)S(1)}, bf16[512,256]{1,0:T(8,128)(2,1)}, u32[]{:S(2)}) %copy-start.3) | copy-done | bytes 262168
  5.2 0.0 copy-start.4
  5.2 0.9 %copy-done.4 = bf16[512,256]{1,0:T(8,128)(2,1)S(1)} copy-done((bf16[512,256]{1,0:T(8,128)(2,1)S(1)}, bf16[512,256]{1,0:T(8,128)(2,1)}, u32[]{:S(2)}) %copy-start.4) | copy-done | bytes 262168
  6.2 0.0 copy-start.5
  6.2 0.9 %copy-done.5 = bf16[512,256]{1,0:T(8,128)(2,1)S(1)} copy-done((bf16[512,256]{1,0:T(8,128)(2,1)S(1)}, bf16[512,256]{1,0:T(8,128)(2,1)}, u32[]{:S(2)}) %copy-start.5) | copy-done | bytes 262168
  7.1 0.0 copy-start.6
  7.1 0.9 %copy-done.6 = bf16[512,256]{1,0:T(8,128)(2,1)S(1)} copy-done((bf16[512,256]{1,0:T(8,128)(2,1)S(1)}, bf16[512,256]{1,0:T(8,128)(2,1)}, u32[]{:S(2)}) %copy-start.6) | copy-done | bytes 262168
  8.1 0.0 copy-start.7
  8.1 0.7 copy-done.7
  8.8 71.1 %hyena.1 = bf16[512,256]{1,0:T(8,128)(2,1)S(1)} custom-call(bf16[512,256]{1,0:T(8,128)(2,1)S(1)} %copy-done.3, bf16[512,256]{1,0:T(8,128)(2,1)S(1)} %copy-done.4, bf16[512,256]{1,0:T(8,128)(2,1)S(1)} %copy-done.5, f32[512,256]{1,0:T(8,128)S(1)} %copy-done.1, f32[1,256]{1,0:T(1,128)S(1)} %bitcast.1, bf16[256,8192]{1,0:T(8,128)(2,1)S(1)} %copy-done, ...), custom_call_target="tpu_custom_call" | custom-call | tf_op jit(solution)/shard_map/hyena/pallas_call | solution.py:289
  79.9 0.7 copy.10
Async XLA Ops:
  0.0 2.2 %copy-start = (bf16[256,8192]{1,0:T(8,128)(2,1)S(1)}, bf16[256,8192]{1,0:T(8,128)(2,1)}, u32[]{:S(2)}) copy-start(bf16[256,8192]{1,0:T(8,128)(2,1)} %w.1) | copy-start | bytes 12582916
  2.2 1.0 %copy-start.1 = (f32[512,256]{1,0:T(8,128)S(1)}, f32[512,256]{1,0:T(8,128)}, u32[]{:S(2)}) copy-start(f32[512,256]{1,0:T(8,128)} %filt.1) | copy-start | bytes 1572868
  3.2 1.0 %copy-start.2 = (bf16[512,512]{1,0:T(8,128)(2,1)S(1)}, bf16[512,512]{1,0:T(8,128)(2,1)}, u32[]{:S(2)}) copy-start(bf16[512,512]{1,0:T(8,128)(2,1)} %constant.4.clone.fwd) | copy-start | bytes 1572868
  4.3 0.9 %copy-start.3 = (bf16[512,256]{1,0:T(8,128)(2,1)S(1)}, bf16[512,256]{1,0:T(8,128)(2,1)}, u32[]{:S(2)}) copy-start(bf16[512,256]{1,0:T(8,128)(2,1)} %gate.1) | copy-start | bytes 786436
  5.2 0.9 %copy-start.4 = (bf16[512,256]{1,0:T(8,128)(2,1)S(1)}, bf16[512,256]{1,0:T(8,128)(2,1)}, u32[]{:S(2)}) copy-start(bf16[512,256]{1,0:T(8,128)(2,1)} %key.1) | copy-start | bytes 786436
  6.2 0.9 %copy-start.5 = (bf16[512,256]{1,0:T(8,128)(2,1)S(1)}, bf16[512,256]{1,0:T(8,128)(2,1)}, u32[]{:S(2)}) copy-start(bf16[512,256]{1,0:T(8,128)(2,1)} %value.1) | copy-start | bytes 786436
  7.1 0.9 %copy-start.6 = (bf16[512,256]{1,0:T(8,128)(2,1)S(1)}, bf16[512,256]{1,0:T(8,128)(2,1)}, u32[]{:S(2)}) copy-start(bf16[512,256]{1,0:T(8,128)(2,1)} %constant.5.clone.bwd) | copy-start | bytes 786436
  8.1 0.7 copy-start.7
where the time goes:
time: 81.1 us; the launch traced here: 80.6 us
  Pallas kernels  71.1 us (88%)
  local copies, waits for them, and re-layouts  9.45 us (12%)
    pallas_call x1, Pallas kernels, body(): pl.pallas_call(kernel, out_shape=jax.ShapeDtypeStruct((POS, CHAN), BF16),...  71.1 us
    unnamed x17, local copies, waits for them, and re-layouts  9.45 us

commit v1 on v0

v1 whole, which is shorter than its diff:
```python
import functools

import jax
import jax.numpy as jnp
import numpy as np
from jax import lax
from jax.experimental import pallas as pl
from jax.experimental.pallas import tpu as pltpu
from jax.sharding import PartitionSpec as P

MESH = pl.DeviceIdType.MESH
F32 = jnp.float32
BF16 = jnp.bfloat16

CTX = 8
POS = 512
CHAN = 256
SUB = CHAN // CTX
BLOCK = 256
BLOCKS = 16
PIECE = 128
RING = 8
ORDER = (4, 3, 5, 2, 6, 1, 7, 0)
SHARE = CHAN // 4


def dot(a, b):
    return jnp.dot(a, b, preferred_element_type=F32)


class Move:
    def __init__(self, copy, log):
        self.copy, self.landed, self.remote = copy, False, copy.is_remote
        copy.start()
        log.append(self)

    def land(self):
        self.landed = True
        if self.remote:
            self.copy.wait_recv()
        else:
            self.copy.wait()

    def leave(self):
        if self.remote:
            self.copy.wait_send()


def tables():
    theta = np.pi * (2 * np.arange(BLOCK) + 1) / (2 * BLOCK)
    at = np.arange(-BLOCK, BLOCK)[:, None] * theta[None, :]
    forward = np.concatenate((np.cos(at), -np.sin(at)), axis=1)
    back_at = theta[:, None] * np.arange(BLOCK)[None, :]
    backward = np.concatenate((np.cos(back_at), -np.sin(back_at)), axis=0) / BLOCK
    return jnp.asarray(forward, BF16), jnp.asarray(backward, BF16)


def kernel(
    gate_h,
    key_h,
    value_h,
    filt_h,
    skip,
    w,
    fwd_h,
    bwd_h,
    out,
    gate,
    key,
    value,
    filt,
    fwd,
    bwd,
    tsend,
    trecv,
    sbuf,
    hbuf,
    zbuf,
    csend,
    crecv,
    gall,
    wbuf,
    rsend,
    rrecv,
    t_ss,
    t_rs,
    c_ss,
    c_rs,
    g_ss,
    g_rs,
    own_s,
    wc_ss,
    wc_rs,
    wy_ss,
    wy_rs,
    wx_ss,
    wx_rs,
    r_ss,
    r_rs,
    loc_s,
    in_s,
):
    log = []
    i = lax.axis_index("ctx")
    j = lax.axis_index("ch")
    x, lo = i // 2, i % 2
    z, q = j // 4, j % 4
    hi, core = q // 2, q % 2

    def remote(src, dst, ss, rs, device):
        copy = pltpu.make_async_remote_copy(
            src_ref=src, dst_ref=dst, send_sem=ss, recv_sem=rs, device_id=device, device_id_type=MESH
        )
        return Move(copy, log)

    def local(src, dst, sem):
        return Move(pltpu.make_async_copy(src, dst, sem), log)

    pairs = ((key_h, key), (value_h, value), (filt_h, filt), (fwd_h, fwd), (bwd_h, bwd), (gate_h, gate))
    key_in, value_in, filt_in, fwd_in, bwd_in, gate_in = [
        local(src, dst, in_s.at[n]) for n, (src, dst) in enumerate(pairs)
    ]

    share = pl.ds(pl.multiple_of(x * SHARE, SHARE), SHARE)

    def w_cols(n, high, cor, rows):
        at = (((z + ORDER[n]) % RING) * 4 + high * 2 + cor) * CHAN
        return w.at[rows, pl.ds(pl.multiple_of(at, CHAN), CHAN)]

    barrier = pltpu.get_barrier_semaphore()
    friends = [((i + d) % CTX, j) for d in range(1, CTX)]
    sibling = (i, z * 4 + hi * 2 + 1 - core)
    across = (i, z * 4 + (q + 2) % 4)
    friends += [sibling, across]
    friends += [(i, ((z + d) % RING) * 4 + q) for d in (1, RING - 1)]
    friends += [(x * 2 + 1 - lo, z * 4 + (1 - hi) * 2 + c) for c in range(2)]
    for friend in friends:
        pl.semaphore_signal(barrier, inc=1, device_id=friend, device_id_type=MESH)

    key_in.land()
    value_in.land()
    signal = key[...].astype(F32) * value[...].astype(F32)
    tsend[0] = signal.T.astype(BF16)
    pl.semaphore_wait(barrier, len(friends))

    def spread(t):
        copies = []
        for d in range(1, CTX):
            to = (i + d) % CTX
            rows = pl.ds(pl.multiple_of(to * SUB, SUB), SUB)
            copies.append(remote(tsend.at[t, rows], trecv.at[t, i], t_ss.at[t, d - 1], t_rs.at[t, d - 1], (to, j)))
        rows = pl.ds(pl.multiple_of(i * SUB, SUB), SUB)
        copies.append(local(tsend.at[t, rows], trecv.at[t, i], loc_s.at[t]))
        return copies

    sig_copies = spread(0)
    filt_in.land()
    tsend[1] = filt[...].T.astype(BF16)
    fil_copies = spread(1)

    wy, wc, own_w = [], [], []
    for n in range(RING):
        both = []
        for m in range(2):
            c = (core + m) % 2
            target = (x * 2 + 1 - lo, z * 4 + (1 - hi) * 2 + c)
            src = w_cols(n, 1 - hi, c, share)
            both.append(remote(src, wbuf.at[n, q, share], wy_ss.at[n, m], wy_rs.at[n, m], target))
        wy.append(both)
    every = pl.ds(0, CHAN)
    for n in range(RING):
        own_w.append(local(w_cols(n, hi, core, every), wbuf.at[n, q], own_s.at[n]))
        wc.append(remote(w_cols(n, hi, 1 - core, every), wbuf.at[n, q], wc_ss.at[n], wc_rs.at[n], sibling))
    wx = {}

    def along_x(g, first, last):
        for n in range(first, last):
            for copy in wy[n]:
                copy.land()
        block = wbuf.at[pl.ds(first, last - first), pl.ds((1 - hi) * 2, 2), share]
        for d in (1, 3, 2):
            target = (((x + d) % 4) * 2 + lo, j)
            copy = remote(block, block, wx_ss.at[g, d - 1], wx_rs.at[g, d - 1], target)
            for n in range(first, last):
                wx.setdefault(n, []).append(copy)

    fwd_in.land()
    for copy in sig_copies:
        copy.land()
    for h in range(2):
        lhs = trecv[0, :, :, h * BLOCK : (h + 1) * BLOCK].reshape(CTX * SUB, BLOCK)
        sbuf[h] = dot(lhs, fwd[BLOCK:, :])
    for copy in fil_copies:
        copy.land()
    hbuf[1] = dot(trecv[1].reshape(CTX * SUB, POS), fwd[...])
    hbuf[0] = dot(trecv[1, :, :, :BLOCK].reshape(CTX * SUB, BLOCK), fwd[BLOCK:, :])
    hbuf[0, SUB:, :] += dot(trecv[1, : CTX - 1, :, BLOCK:].reshape((CTX - 1) * SUB, BLOCK), fwd[:BLOCK, :])

    along_x(0, 0, 1)
    bwd_in.land()
    mine_rows = pl.ds(pl.multiple_of(i * SUB, SUB), SUB)
    back = []
    for h in range(2):
        @pl.loop(0, (SUB // 8) * (BLOCK // 128))
        def _(t):
            row0 = (t // 2) * 8
            lane_re = pl.multiple_of((t % 2) * 128, 128)
            lane_im = pl.multiple_of(BLOCK + (t % 2) * 128, 128)

            def at(a):
                return pl.ds(pl.multiple_of((a // 2) * SUB + row0, 8), 8)

            def take(ref, a):
                return ref[a % 2, at(a), pl.ds(lane_re, 128)], ref[a % 2, at(a), pl.ds(lane_im, 128)]

            for a in range(h, BLOCKS, 2):
                re = im = None
                for d in range(a + 1):
                    sr, si = take(sbuf, a - d)
                    hr, hm = take(hbuf, d)
                    pr = sr * hr - si * hm
                    pm = sr * hm + si * hr
                    re = pr if re is None else re + pr
                    im = pm if im is None else im + pm
                zbuf[h, at(a), pl.ds(lane_re, 128)] = re
                zbuf[h, at(a), pl.ds(lane_im, 128)] = im

        csend[h] = dot(zbuf[h].astype(BF16), bwd[...]).astype(BF16)
        copies = []
        for d in range(1, CTX):
            to = (i + d) % CTX
            rows = pl.ds(pl.multiple_of(to * SUB, SUB), SUB)
            copies.append(
                remote(csend.at[h, rows], crecv.at[h, mine_rows], c_ss.at[h, d - 1], c_rs.at[h, d - 1], (to, j))
            )
        copies.append(local(csend.at[h, mine_rows], crecv.at[h, mine_rows], loc_s.at[2 + h]))
        back.append(copies)

    gate_in.land()
    cross, beside, passed = [], [], []
    for h in range(2):
        rows = pl.ds(h * BLOCK, BLOCK)
        for copy in back[h]:
            copy.land()
        convolved = crecv[h].astype(F32).T
        signal = key[rows, :].astype(F32) * value[rows, :].astype(F32)
        gall[q, rows] = ((convolved + skip[...] * signal) * gate[rows, :].astype(F32)).astype(BF16)
        block = gall.at[q, rows]
        cross.append(remote(block, block, g_ss.at[h, 0], g_rs.at[h, 0], across))
        beside.append(remote(block, block, g_ss.at[h, 1], g_rs.at[h, 1], sibling))
    along_x(1, 1, 3)

    def gathered(h):
        cross[h].land()
        block = gall.at[(q + 2) % 4, pl.ds(h * BLOCK, BLOCK)]
        passed.append(remote(block, block, g_ss.at[h, 2], g_rs.at[h, 2], sibling))
        beside[h].land()
        passed[h].land()

    ready = set()

    def partial(far, r):
        n = ORDER.index(far)
        if n not in ready:
            ready.add(n)
            for copy in [own_w[n], wc[n]] + wx[n]:
                if not copy.landed:
                    copy.land()
        rows = slice(r * PIECE, (r + 1) * PIECE)
        total = dot(gall[0, rows], wbuf[n, 0])
        for k in range(1, 4):
            total += dot(gall[k, rows], wbuf[n, k])
        return total

    turns = []
    for way in range(2):
        near, far = (way, 2 + way), (1 - way, 3 - way)
        turn = [(0, near[0]), (1, far[0]), (0, near[1]), (1, far[1]), (1, near[0]), (1, near[1])]
        for step in (2, 3):
            turn += [(step, r) for r in far + near]
        turns.append(turn)
    sums = {}
    for n in range(len(turns[0])):
        if n == 0:
            gathered(0)
        if n == 2:
            gathered(1)
            along_x(2, 3, 5)
        if n == 6:
            along_x(3, 5, 8)
        for way, near in ((0, 1), (1, RING - 1)):
            step, r = turns[way][n]
            rows = pl.ds(r * PIECE, PIECE)
            total = partial(4 - step if way == 0 else 4 + step, r)
            if (way, step - 1, r) in sums:
                sums[way, step - 1, r].land()
                total = total + rrecv[way, step - 1, rows].astype(F32)
            rsend[way, step, rows] = total.astype(BF16)
            sums[way, step, r] = remote(
                rsend.at[way, step, rows],
                rrecv.at[way, step, rows],
                r_ss.at[way, step, r],
                r_rs.at[way, step, r],
                (i, ((z + near) % RING) * 4 + q),
            )
    for r in range(POS // PIECE):
        rows = pl.ds(r * PIECE, PIECE)
        total = partial(0, r)
        for way in range(2):
            sums[way, 3, r].land()
            total = total + rrecv[way, 3, rows].astype(F32)
        out[rows, :] = total.astype(BF16)

    for copy in log:
        copy.leave()


def body(gate, key, value, filt, skip, w, fwd, bwd):
    vmem = pl.BlockSpec(memory_space=pltpu.VMEM)
    hbm = pl.BlockSpec(memory_space=pltpu.HBM)
    dma = pltpu.SemaphoreType.DMA
    return pl.pallas_call(
        kernel,
        out_shape=jax.ShapeDtypeStruct((POS, CHAN), BF16),
        in_specs=[hbm] * 4 + [vmem] + [hbm] * 3,
        out_specs=vmem,
        scratch_shapes=[
            pltpu.VMEM((POS, CHAN), BF16),
            pltpu.VMEM((POS, CHAN), BF16),
            pltpu.VMEM((POS, CHAN), BF16),
            pltpu.VMEM((POS, CHAN), F32),
            pltpu.VMEM((2 * BLOCK, 2 * BLOCK), BF16),
            pltpu.VMEM((2 * BLOCK, BLOCK), BF16),
            pltpu.VMEM((2, CHAN, POS), BF16),
            pltpu.VMEM((2, CTX, SUB, POS), BF16),
            pltpu.VMEM((2, CHAN, 2 * BLOCK), F32),
            pltpu.VMEM((2, CHAN, 2 * BLOCK), F32),
            pltpu.VMEM((2, CHAN, 2 * BLOCK), F32),
            pltpu.VMEM((2, CHAN, BLOCK), BF16),
            pltpu.VMEM((2, CHAN, BLOCK), BF16),
            pltpu.VMEM((4, POS, CHAN), BF16),
            pltpu.VMEM((RING, 4, CHAN, CHAN), BF16),
            pltpu.VMEM((2, 4, POS, CHAN), BF16),
            pltpu.VMEM((2, 4, POS, CHAN), BF16),
            dma((2, CTX - 1)),
            dma((2, CTX - 1)),
            dma((2, CTX - 1)),
            dma((2, CTX - 1)),
            dma((2, 3)),
            dma((2, 3)),
            dma((RING,)),
            dma((RING,)),
            dma((RING,)),
            dma((RING, 2)),
            dma((RING, 2)),
            dma((4, 3)),
            dma((4, 3)),
            dma((2, 4, POS // PIECE)),
            dma((2, 4, POS // PIECE)),
            dma((4,)),
            dma((6,)),
        ],
        compiler_params=pltpu.CompilerParams(
            collective_id=0, has_side_effects=True, vmem_limit_bytes=64 * 1024 * 1024
        ),
        name="hyena",
    )(gate, key, value, filt, skip.reshape(1, CHAN), w, fwd, bwd)


def solution(mesh):
    mapped = jax.shard_map(
        body,
        mesh=mesh,
        in_specs=(P("ctx", "ch"),) * 4 + (P("ch"), P("ch", None), P(), P()),
        out_specs=P("ctx", "ch"),
        check_vma=False,
    )

    def run(out_gate, key_proj, value_proj, filters, skip_gain, out_weight):
        return mapped(out_gate, key_proj, value_proj, filters, skip_gain, out_weight, *tables())

    return run
```

time: 81.1 us -> 65.2 us (0.80)
  local copies, waits for them, and re-layouts: 9.45 us -> 1.67 us
  Pallas kernels: 71.1 us -> 63.4 us
    unnamed x17 -> x1, local copies, waits for them, and re-layouts: 9.45 us -> 1.67 us
    pallas_call x1, Pallas kernels: 71.1 us -> 63.4 us  [body(): pl.pallas_call(kernel, out_shape=jax.ShapeDtypeStruct((POS, CHAN), BF16),...]
where the time goes in v1:
time: 65.2 us; the launch traced here: 65.1 us
  Pallas kernels  63.4 us (97%)
  local copies, waits for them, and re-layouts  1.67 us (3%)
    pallas_call x1, Pallas kernels, body(): pl.pallas_call(kernel, out_shape=jax.ShapeDtypeStruct((POS, CHAN), BF16),...  63.4 us
    unnamed x1, local copies, waits for them, and re-layouts  1.67 us

profile of v1, /device:TPU:1, one launch (start us, length us, event | category | flops | bytes accessed | tf_op | source)
XLA Modules:
  0.0 65.1 jit_solution(7922302956146235297)
XLA Ops:
  0.0 63.4 %hyena.1 = bf16[512,256]{1,0:T(8,128)(2,1)} custom-call(bf16[512,256]{1,0:T(8,128)(2,1)} %gate_h.1, bf16[512,256]{1,0:T(8,128)(2,1)} %key_h.1, bf16[512,256]{1,0:T(8,128)(2,1)} %value_h.1, f32[512,256]{1,0:T(8,128)} %filt_h.1, f32[1,256]{1,0:T(1,128)} %bitcast.1, bf16[256,8192]{1,0:T(8,128)(2,1)} %w.1, bf16[512,512]{1,0:T(8,128)(2,1)} %constant.4.clone.fwd_h, ...), custom_call_target="tpu_custom_call" | custom-call | tf_op jit(solution)/shard_map/hyena/pallas_call | solution.py:322
  63.4 1.7 %copy.10 = bf16[512,256]{1,0:T(8,128)(2,1)} copy(bf16[512,256]{1,0:T(8,128)(2,1)} %hyena.1) | data formatting | bytes 524288

commit v2 on v1

--- a/solution.py
+++ b/solution.py
@@ -22,6 +22,7 @@
 RING = 8
 ORDER = (4, 3, 5, 2, 6, 1, 7, 0)
 SHARE = CHAN // 4
+TWICE = (1, 2)
 
 
 def dot(a, b):
@@ -61,7 +62,7 @@
     value_h,
     filt_h,
     skip,
-    w,
+    w_h,
     fwd_h,
     bwd_h,
     out,
@@ -71,6 +72,7 @@
     filt,
     fwd,
     bwd,
+    w,
     tsend,
     trecv,
     sbuf,
@@ -80,6 +82,7 @@
     crecv,
     gall,
     wbuf,
+    pbuf,
     rsend,
     rrecv,
     t_ss,
@@ -88,7 +91,6 @@
     c_rs,
     g_ss,
     g_rs,
-    own_s,
     wc_ss,
     wc_rs,
     wy_ss,
@@ -116,12 +118,12 @@
     def local(src, dst, sem):
         return Move(pltpu.make_async_copy(src, dst, sem), log)
 
-    pairs = ((key_h, key), (value_h, value), (filt_h, filt), (fwd_h, fwd), (bwd_h, bwd), (gate_h, gate))
-    key_in, value_in, filt_in, fwd_in, bwd_in, gate_in = [
+    pairs = ((key_h, key), (value_h, value), (filt_h, filt), (fwd_h, fwd), (bwd_h, bwd), (gate_h, gate), (w_h, w))
+    key_in, value_in, filt_in, fwd_in, bwd_in, gate_in, w_in = [
         local(src, dst, in_s.at[n]) for n, (src, dst) in enumerate(pairs)
     ]
 
-    share = pl.ds(pl.multiple_of(x * SHARE, SHARE), SHARE)
+    shares = [pl.ds(pl.multiple_of((x + d) % 4 * SHARE, SHARE), SHARE) for d in range(2)]
 
     def w_cols(n, high, cor, rows):
         at = (((z + ORDER[n]) % RING) * 4 + high * 2 + cor) * CHAN
@@ -158,27 +160,33 @@
     tsend[1] = filt[...].T.astype(BF16)
     fil_copies = spread(1)
 
-    wy, wc, own_w = [], [], []
-    for n in range(RING):
-        both = []
-        for m in range(2):
-            c = (core + m) % 2
-            target = (x * 2 + 1 - lo, z * 4 + (1 - hi) * 2 + c)
-            src = w_cols(n, 1 - hi, c, share)
-            both.append(remote(src, wbuf.at[n, q, share], wy_ss.at[n, m], wy_rs.at[n, m], target))
-        wy.append(both)
+    w_in.land()
+    wy, wc = {}, []
+
+    def along_y(first, last):
+        for n in range(first, last):
+            wy[n] = []
+            for m in range(2):
+                c = (core + m) % 2
+                target = (x * 2 + 1 - lo, z * 4 + (1 - hi) * 2 + c)
+                for d, rows in enumerate(shares if n in TWICE else shares[:1]):
+                    src = w_cols(n, 1 - hi, c, rows)
+                    wy[n].append(remote(src, wbuf.at[n, q, rows], wy_ss.at[n, m, d], wy_rs.at[n, m, d], target))
+
+    along_y(0, RING)
     every = pl.ds(0, CHAN)
-    for n in range(RING):
-        own_w.append(local(w_cols(n, hi, core, every), wbuf.at[n, q], own_s.at[n]))
-        wc.append(remote(w_cols(n, hi, 1 - core, every), wbuf.at[n, q], wc_ss.at[n], wc_rs.at[n], sibling))
     wx = {}
 
     def along_x(g, first, last):
         for n in range(first, last):
             for copy in wy[n]:
                 copy.land()
-        block = wbuf.at[pl.ds(first, last - first), pl.ds((1 - hi) * 2, 2), share]
-        for d in (1, 3, 2):
+        if first in TWICE:
+            plan = ((1, shares[0]), (3, shares[1]))
+        else:
+            plan = ((1, shares[0]), (3, shares[0]), (2, shares[0]))
+        for d, rows in plan:
+            block = wbuf.at[pl.ds(first, last - first), pl.ds((1 - hi) * 2, 2), rows]
             target = (((x + d) % 4) * 2 + lo, j)
             copy = remote(block, block, wx_ss.at[g, d - 1], wx_rs.at[g, d - 1], target)
             for n in range(first, last):
@@ -235,6 +243,9 @@
             )
         copies.append(local(csend.at[h, mine_rows], crecv.at[h, mine_rows], loc_s.at[2 + h]))
         back.append(copies)
+
+    for n in range(RING):
+        wc.append(remote(w_cols(n, hi, 1 - core, every), wbuf.at[n, q], wc_ss.at[n], wc_rs.at[n], sibling))
 
     gate_in.land()
     cross, beside, passed = [], [], []
@@ -249,6 +260,8 @@
         cross.append(remote(block, block, g_ss.at[h, 0], g_rs.at[h, 0], across))
         beside.append(remote(block, block, g_ss.at[h, 1], g_rs.at[h, 1], sibling))
     along_x(1, 1, 3)
+    along_x(2, 3, 5)
+    along_x(3, 5, 8)
 
     def gathered(h):
         cross[h].land()
@@ -259,18 +272,19 @@
 
     ready = set()
 
-    def partial(far, r):
+    def partial(far, first, count):
         n = ORDER.index(far)
         if n not in ready:
             ready.add(n)
-            for copy in [own_w[n], wc[n]] + wx[n]:
+            for copy in [wc[n]] + wx[n]:
                 if not copy.landed:
                     copy.land()
-        rows = slice(r * PIECE, (r + 1) * PIECE)
-        total = dot(gall[0, rows], wbuf[n, 0])
+        rows = pl.ds(first, count)
+        total = dot(gall[q, rows], w_cols(n, hi, core, every)[...])
         for k in range(1, 4):
-            total += dot(gall[k, rows], wbuf[n, k])
-        return total
+            at = (q + k) % 4
+            total += dot(gall[at, rows], wbuf[n, at])
+        pbuf[n, rows] = total
 
     turns = []
     for way in range(2):
@@ -280,18 +294,20 @@
             turn += [(step, r) for r in far + near]
         turns.append(turn)
     sums = {}
+    ahead = {4: (2,), 6: (6,), 8: (1,), 10: (7,), 12: (0,)}
     for n in range(len(turns[0])):
-        if n == 0:
-            gathered(0)
-        if n == 2:
-            gathered(1)
-            along_x(2, 3, 5)
-        if n == 6:
-            along_x(3, 5, 8)
+        if n in (0, 2):
+            gathered(n // 2)
+            partial(4, n // 2 * BLOCK, BLOCK)
+        for far in ahead.get(n, ()):
+            partial(far, 0, POS)
         for way, near in ((0, 1), (1, RING - 1)):
             step, r = turns[way][n]
+            far = 4 - step if way == 0 else 4 + step
+            if n in (1, 3):
+                partial(far, n // 2 * BLOCK, BLOCK)
             rows = pl.ds(r * PIECE, PIECE)
-            total = partial(4 - step if way == 0 else 4 + step, r)
+            total = pbuf[ORDER.index(far), rows]
             if (way, step - 1, r) in sums:
                 sums[way, step - 1, r].land()
                 total = total + rrecv[way, step - 1, rows].astype(F32)
@@ -303,9 +319,9 @@
                 r_rs.at[way, step, r],
                 (i, ((z + near) % RING) * 4 + q),
             )
-    for r in range(POS // PIECE):
+    for r in (1, 3, 0, 2):
         rows = pl.ds(r * PIECE, PIECE)
-        total = partial(0, r)
+        total = pbuf[ORDER.index(0), rows]
         for way in range(2):
             sums[way, 3, r].land()
             total = total + rrecv[way, 3, rows].astype(F32)
@@ -331,6 +347,7 @@
             pltpu.VMEM((POS, CHAN), F32),
             pltpu.VMEM((2 * BLOCK, 2 * BLOCK), BF16),
             pltpu.VMEM((2 * BLOCK, BLOCK), BF16),
+            pltpu.VMEM((CHAN, RING * 4 * CHAN), BF16),
             pltpu.VMEM((2, CHAN, POS), BF16),
             pltpu.VMEM((2, CTX, SUB, POS), BF16),
             pltpu.VMEM((2, CHAN, 2 * BLOCK), F32),
@@ -340,6 +357,7 @@
             pltpu.VMEM((2, CHAN, BLOCK), BF16),
             pltpu.VMEM((4, POS, CHAN), BF16),
             pltpu.VMEM((RING, 4, CHAN, CHAN), BF16),
+            pltpu.VMEM((RING, POS, CHAN), F32),
             pltpu.VMEM((2, 4, POS, CHAN), BF16),
             pltpu.VMEM((2, 4, POS, CHAN), BF16),
             dma((2, CTX - 1)),
@@ -350,15 +368,14 @@
             dma((2, 3)),
             dma((RING,)),
             dma((RING,)),
-            dma((RING,)),
-            dma((RING, 2)),
-            dma((RING, 2)),
+            dma((RING, 2, 2)),
+            dma((RING, 2, 2)),
             dma((4, 3)),
             dma((4, 3)),
             dma((2, 4, POS // PIECE)),
             dma((2, 4, POS // PIECE)),
             dma((4,)),
-            dma((6,)),
+            dma((7,)),
         ],
         compiler_params=pltpu.CompilerParams(
             collective_id=0, has_side_effects=True, vmem_limit_bytes=64 * 1024 * 1024

time: 65.2 us -> 60.8 us (0.933)
  Pallas kernels: 63.4 us -> 59 us
    pallas_call x1, Pallas kernels: 63.4 us -> 59 us  [body(): pl.pallas_call(kernel, out_shape=jax.ShapeDtypeStruct((POS, CHAN), BF16),...]
where the time goes in v2:
time: 60.8 us; the launch traced here: 60.7 us
  Pallas kernels  59 us (97%)
  local copies, waits for them, and re-layouts  1.67 us (3%)
    pallas_call x1, Pallas kernels, body(): pl.pallas_call(kernel, out_shape=jax.ShapeDtypeStruct((POS, CHAN), BF16),...  59 us
    unnamed x1, local copies, waits for them, and re-layouts  1.67 us

profile of v2, /device:TPU:1, one launch (start us, length us, event | category | flops | bytes accessed | tf_op | source)
XLA Modules:
  0.0 60.7 jit_solution(13842767055878516806)
XLA Ops:
  0.0 59.0 %hyena.1 = bf16[512,256]{1,0:T(8,128)(2,1)} custom-call(bf16[512,256]{1,0:T(8,128)(2,1)} %gate_h.1, bf16[512,256]{1,0:T(8,128)(2,1)} %key_h.1, bf16[512,256]{1,0:T(8,128)(2,1)} %value_h.1, f32[512,256]{1,0:T(8,128)} %filt_h.1, f32[1,256]{1,0:T(1,128)} %bitcast.1, bf16[256,8192]{1,0:T(8,128)(2,1)} %w_h.1, bf16[512,512]{1,0:T(8,128)(2,1)} %constant.4.clone.fwd_h, ...), custom_call_target="tpu_custom_call" | custom-call | tf_op jit(solution)/shard_map/hyena/pallas_call | solution.py:338
  59.0 1.7 %copy.10 = bf16[512,256]{1,0:T(8,128)(2,1)} copy(bf16[512,256]{1,0:T(8,128)(2,1)} %hyena.1) | data formatting | bytes 524288

commit v3 on v2

--- a/solution.py
+++ b/solution.py
@@ -15,6 +15,7 @@
 CTX = 8
 POS = 512
 CHAN = 256
+FARTHEST = (4, 5, 3, 2, 6, 1, 7)
 SUB = CHAN // CTX
 BLOCK = 256
 BLOCKS = 16
@@ -143,11 +144,13 @@
     value_in.land()
     signal = key[...].astype(F32) * value[...].astype(F32)
     tsend[0] = signal.T.astype(BF16)
+    filt_in.land()
+    tsend[1] = filt[...].T.astype(BF16)
     pl.semaphore_wait(barrier, len(friends))
 
     def spread(t):
         copies = []
-        for d in range(1, CTX):
+        for d in FARTHEST:
             to = (i + d) % CTX
             rows = pl.ds(pl.multiple_of(to * SUB, SUB), SUB)
             copies.append(remote(tsend.at[t, rows], trecv.at[t, i], t_ss.at[t, d - 1], t_rs.at[t, d - 1], (to, j)))
@@ -156,8 +159,6 @@
         return copies
 
     sig_copies = spread(0)
-    filt_in.land()
-    tsend[1] = filt[...].T.astype(BF16)
     fil_copies = spread(1)
 
     w_in.land()
@@ -235,12 +236,14 @@
 
         csend[h] = dot(zbuf[h].astype(BF16), bwd[...]).astype(BF16)
         copies = []
-        for d in range(1, CTX):
+        for d in FARTHEST:
             to = (i + d) % CTX
             rows = pl.ds(pl.multiple_of(to * SUB, SUB), SUB)
             copies.append(
                 remote(csend.at[h, rows], crecv.at[h, mine_rows], c_ss.at[h, d - 1], c_rs.at[h, d - 1], (to, j))
             )
+        if h == 0:
+            along_x(1, 1, 3)
         copies.append(local(csend.at[h, mine_rows], crecv.at[h, mine_rows], loc_s.at[2 + h]))
         back.append(copies)
 
@@ -256,19 +259,17 @@
         convolved = crecv[h].astype(F32).T
         signal = key[rows, :].astype(F32) * value[rows, :].astype(F32)
         gall[q, rows] = ((convolved + skip[...] * signal) * gate[rows, :].astype(F32)).astype(BF16)
-        block = gall.at[q, rows]
-        cross.append(remote(block, block, g_ss.at[h, 0], g_rs.at[h, 0], across))
-        beside.append(remote(block, block, g_ss.at[h, 1], g_rs.at[h, 1], sibling))
-    along_x(1, 1, 3)
+        for r in (2 * h, 2 * h + 1):
+            block = gall.at[q, pl.ds(r * PIECE, PIECE)]
+            cross.append(remote(block, block, g_ss.at[r, 0], g_rs.at[r, 0], across))
+            beside.append(remote(block, block, g_ss.at[r, 1], g_rs.at[r, 1], sibling))
     along_x(2, 3, 5)
     along_x(3, 5, 8)
 
-    def gathered(h):
-        cross[h].land()
-        block = gall.at[(q + 2) % 4, pl.ds(h * BLOCK, BLOCK)]
-        passed.append(remote(block, block, g_ss.at[h, 2], g_rs.at[h, 2], sibling))
-        beside[h].land()
-        passed[h].land()
+    def hand_on(r):
+        cross[r].land()
+        block = gall.at[(q + 2) % 4, pl.ds(r * PIECE, PIECE)]
+        passed.append(remote(block, block, g_ss.at[r, 2], g_rs.at[r, 2], sibling))
 
     ready = set()
 
@@ -289,23 +290,27 @@
     turns = []
     for way in range(2):
         near, far = (way, 2 + way), (1 - way, 3 - way)
-        turn = [(0, near[0]), (1, far[0]), (0, near[1]), (1, far[1]), (1, near[0]), (1, near[1])]
+        turn = [((r + way) % 2, r) for r in range(4)] + [(1, r) for r in near]
         for step in (2, 3):
             turn += [(step, r) for r in far + near]
         turns.append(turn)
     sums = {}
     ahead = {4: (2,), 6: (6,), 8: (1,), 10: (7,), 12: (0,)}
     for n in range(len(turns[0])):
-        if n in (0, 2):
-            gathered(n // 2)
-            partial(4, n // 2 * BLOCK, BLOCK)
+        if n == 0:
+            hand_on(0)
+        if n < 4:
+            beside[n].land()
+            passed[n].land()
         for far in ahead.get(n, ()):
             partial(far, 0, POS)
         for way, near in ((0, 1), (1, RING - 1)):
             step, r = turns[way][n]
             far = 4 - step if way == 0 else 4 + step
-            if n in (1, 3):
-                partial(far, n // 2 * BLOCK, BLOCK)
+            if n < 6:
+                partial(far, r * PIECE, PIECE)
+            if way == 1 and n < 3:
+                hand_on(n + 1)
             rows = pl.ds(r * PIECE, PIECE)
             total = pbuf[ORDER.index(far), rows]
             if (way, step - 1, r) in sums:
@@ -364,8 +369,8 @@
             dma((2, CTX - 1)),
             dma((2, CTX - 1)),
             dma((2, CTX - 1)),
-            dma((2, 3)),
-            dma((2, 3)),
+            dma((4, 3)),
+            dma((4, 3)),
             dma((RING,)),
             dma((RING,)),
             dma((RING, 2, 2)),

time: 60.8 us -> 60.1 us (0.988)
  the two profiles are of different devices: /device:TPU:1 before, /device:TPU:24 now
where the time goes in v3:
time: 60.1 us; the launch traced here: 60 us
  Pallas kernels  58.3 us (97%)
  local copies, waits for them, and re-layouts  1.67 us (3%)
    pallas_call x1, Pallas kernels, body(): pl.pallas_call(kernel, out_shape=jax.ShapeDtypeStruct((POS, CHAN), BF16),...  58.3 us
    unnamed x1, local copies, waits for them, and re-layouts  1.67 us

profile of v3, /device:TPU:24, one launch (start us, length us, event | category | flops | bytes accessed | tf_op | source)
XLA Modules:
  0.0 60.0 jit_solution(14915977052019623787)
XLA Ops:
  0.0 58.3 %hyena.1 = bf16[512,256]{1,0:T(8,128)(2,1)} custom-call(bf16[512,256]{1,0:T(8,128)(2,1)} %gate_h.1, bf16[512,256]{1,0:T(8,128)(2,1)} %key_h.1, bf16[512,256]{1,0:T(8,128)(2,1)} %value_h.1, f32[512,256]{1,0:T(8,128)} %filt_h.1, f32[1,256]{1,0:T(1,128)} %bitcast.1, bf16[256,8192]{1,0:T(8,128)(2,1)} %w_h.1, bf16[512,512]{1,0:T(8,128)(2,1)} %constant.4.clone.fwd_h, ...), custom_call_target="tpu_custom_call" | custom-call | tf_op jit(solution)/shard_map/hyena/pallas_call | solution.py:343
  58.3 1.7 %copy.10 = bf16[512,256]{1,0:T(8,128)(2,1)} copy(bf16[512,256]{1,0:T(8,128)(2,1)} %hyena.1) | data formatting | bytes 524288

commit v4 on v3

--- a/solution.py
+++ b/solution.py
@@ -206,6 +206,8 @@
     hbuf[0, SUB:, :] += dot(trecv[1, : CTX - 1, :, BLOCK:].reshape((CTX - 1) * SUB, BLOCK), fwd[:BLOCK, :])
 
     along_x(0, 0, 1)
+    gate_in.land()
+    pbuf[0] = skip[...] * (key[...].astype(F32) * value[...].astype(F32)) * gate[...].astype(F32)
     bwd_in.land()
     mine_rows = pl.ds(pl.multiple_of(i * SUB, SUB), SUB)
     back = []
@@ -250,20 +252,19 @@
     for n in range(RING):
         wc.append(remote(w_cols(n, hi, 1 - core, every), wbuf.at[n, q], wc_ss.at[n], wc_rs.at[n], sibling))
 
-    gate_in.land()
     cross, beside, passed = [], [], []
     for h in range(2):
         rows = pl.ds(h * BLOCK, BLOCK)
         for copy in back[h]:
             copy.land()
+        if h == 1:
+            along_x(2, 3, 5)
         convolved = crecv[h].astype(F32).T
-        signal = key[rows, :].astype(F32) * value[rows, :].astype(F32)
-        gall[q, rows] = ((convolved + skip[...] * signal) * gate[rows, :].astype(F32)).astype(BF16)
+        gall[q, rows] = (convolved * gate[rows, :].astype(F32) + pbuf[0, rows]).astype(BF16)
         for r in (2 * h, 2 * h + 1):
             block = gall.at[q, pl.ds(r * PIECE, PIECE)]
             cross.append(remote(block, block, g_ss.at[r, 0], g_rs.at[r, 0], across))
             beside.append(remote(block, block, g_ss.at[r, 1], g_rs.at[r, 1], sibling))
-    along_x(2, 3, 5)
     along_x(3, 5, 8)
 
     def hand_on(r):
@@ -295,7 +296,7 @@
             turn += [(step, r) for r in far + near]
         turns.append(turn)
     sums = {}
-    ahead = {4: (2,), 6: (6,), 8: (1,), 10: (7,), 12: (0,)}
+    ahead = {6: (2, 6), 10: (1, 7), 13: (0,)}
     for n in range(len(turns[0])):
         if n == 0:
             hand_on(0)
@@ -342,7 +343,7 @@
     dma = pltpu.SemaphoreType.DMA
     return pl.pallas_call(
         kernel,
-        out_shape=jax.ShapeDtypeStruct((POS, CHAN), BF16),
+        out_shape=pltpu.VMEM((POS, CHAN), BF16),
         in_specs=[hbm] * 4 + [vmem] + [hbm] * 3,
         out_specs=vmem,
         scratch_shapes=[
@@ -383,7 +384,7 @@
             dma((7,)),
         ],
         compiler_params=pltpu.CompilerParams(
-            collective_id=0, has_side_effects=True, vmem_limit_bytes=64 * 1024 * 1024
+            collective_id=0, has_side_effects=True, vmem_limit_bytes=64 * 1024 * 1024 - 1024 * 1024
         ),
         name="hyena",
     )(gate, key, value, filt, skip.reshape(1, CHAN), w, fwd, bwd)

time: 60.1 us -> 57.1 us (0.950)
  the two profiles are of different devices: /device:TPU:24 before, /device:TPU:1 now
where the time goes in v4:
time: 57.1 us; the launch traced here: 56.4 us
  Pallas kernels  55.7 us (98%)
  local copies, waits for them, and re-layouts  0.71 us (1%)
    pallas_call x1, Pallas kernels, body(): pl.pallas_call(kernel, out_shape=pltpu.VMEM((POS, CHAN), BF16), in_specs=...  55.7 us

profile of v4, /device:TPU:1, one launch (start us, length us, event | category | flops | bytes accessed | tf_op | source)
XLA Modules:
  0.0 56.4 jit_solution(13916975099374229908)
XLA Ops:
  0.0 55.7 %hyena.1 = bf16[512,256]{1,0:T(8,128)(2,1)S(1)} custom-call(bf16[512,256]{1,0:T(8,128)(2,1)} %gate_h.1, bf16[512,256]{1,0:T(8,128)(2,1)} %key_h.1, bf16[512,256]{1,0:T(8,128)(2,1)} %value_h.1, f32[512,256]{1,0:T(8,128)} %filt_h.1, f32[1,256]{1,0:T(1,128)} %bitcast.1, bf16[256,8192]{1,0:T(8,128)(2,1)} %w_h.1, bf16[512,512]{1,0:T(8,128)(2,1)} %constant.4.clone.fwd_h, ...), custom_call_target="tpu_custom_call" | custom-call | tf_op jit(solution)/shard_map/hyena/pallas_call | solution.py:344
  55.7 0.7 %copy.10 = bf16[512,256]{1,0:T(8,128)(2,1)} copy(bf16[512,256]{1,0:T(8,128)(2,1)S(1)} %hyena.1) | data formatting | bytes 524288

commit v5 on v4

--- a/solution.py
+++ b/solution.py
@@ -158,8 +158,8 @@
         copies.append(local(tsend.at[t, rows], trecv.at[t, i], loc_s.at[t]))
         return copies
 
+    fil_copies = spread(1)
     sig_copies = spread(0)
-    fil_copies = spread(1)
 
     w_in.land()
     wy, wc = {}, []
@@ -193,21 +193,22 @@
             for n in range(first, last):
                 wx.setdefault(n, []).append(copy)
 
+    gate_in.land()
+    pbuf[0] = skip[...] * (key[...].astype(F32) * value[...].astype(F32)) * gate[...].astype(F32)
+
     fwd_in.land()
+    for copy in fil_copies:
+        copy.land()
+    hbuf[1] = dot(trecv[1].reshape(CTX * SUB, POS), fwd[...])
+    hbuf[0] = dot(trecv[1, :, :, :BLOCK].reshape(CTX * SUB, BLOCK), fwd[BLOCK:, :])
+    hbuf[0, SUB:, :] += dot(trecv[1, : CTX - 1, :, BLOCK:].reshape((CTX - 1) * SUB, BLOCK), fwd[:BLOCK, :])
+
     for copy in sig_copies:
         copy.land()
     for h in range(2):
         lhs = trecv[0, :, :, h * BLOCK : (h + 1) * BLOCK].reshape(CTX * SUB, BLOCK)
         sbuf[h] = dot(lhs, fwd[BLOCK:, :])
-    for copy in fil_copies:
-        copy.land()
-    hbuf[1] = dot(trecv[1].reshape(CTX * SUB, POS), fwd[...])
-    hbuf[0] = dot(trecv[1, :, :, :BLOCK].reshape(CTX * SUB, BLOCK), fwd[BLOCK:, :])
-    hbuf[0, SUB:, :] += dot(trecv[1, : CTX - 1, :, BLOCK:].reshape((CTX - 1) * SUB, BLOCK), fwd[:BLOCK, :])
-
     along_x(0, 0, 1)
-    gate_in.land()
-    pbuf[0] = skip[...] * (key[...].astype(F32) * value[...].astype(F32)) * gate[...].astype(F32)
     bwd_in.land()
     mine_rows = pl.ds(pl.multiple_of(i * SUB, SUB), SUB)
     back = []
@@ -254,18 +255,19 @@
 
     cross, beside, passed = [], [], []
     for h in range(2):
-        rows = pl.ds(h * BLOCK, BLOCK)
         for copy in back[h]:
             copy.land()
         if h == 1:
             along_x(2, 3, 5)
-        convolved = crecv[h].astype(F32).T
-        gall[q, rows] = (convolved * gate[rows, :].astype(F32) + pbuf[0, rows]).astype(BF16)
         for r in (2 * h, 2 * h + 1):
-            block = gall.at[q, pl.ds(r * PIECE, PIECE)]
+            rows = pl.ds(r * PIECE, PIECE)
+            convolved = crecv[h, :, pl.ds(r % 2 * PIECE, PIECE)].astype(F32).T
+            gall[q, rows] = (convolved * gate[rows, :].astype(F32) + pbuf[0, rows]).astype(BF16)
+            block = gall.at[q, rows]
             cross.append(remote(block, block, g_ss.at[r, 0], g_rs.at[r, 0], across))
             beside.append(remote(block, block, g_ss.at[r, 1], g_rs.at[r, 1], sibling))
-    along_x(3, 5, 8)
+    along_x(3, 5, 7)
+    along_x(4, 7, 8)
 
     def hand_on(r):
         cross[r].land()
@@ -376,8 +378,8 @@
             dma((RING,)),
             dma((RING, 2, 2)),
             dma((RING, 2, 2)),
-            dma((4, 3)),
-            dma((4, 3)),
+            dma((5, 3)),
+            dma((5, 3)),
             dma((2, 4, POS // PIECE)),
             dma((2, 4, POS // PIECE)),
             dma((4,)),

time: 57.1 us -> 57 us (level)
  no operation moved by 1% of the time
where the time goes in v5:
time: 57 us; the launch traced here: 56.4 us
  Pallas kernels  55.7 us (98%)
  local copies, waits for them, and re-layouts  0.71 us (1%)
    pallas_call x1, Pallas kernels, body(): pl.pallas_call(kernel, out_shape=pltpu.VMEM((POS, CHAN), BF16), in_specs=...  55.7 us

profile of v5, /device:TPU:1, one launch (start us, length us, event | category | flops | bytes accessed | tf_op | source)
XLA Modules:
  0.0 56.4 jit_solution(10023194617902750745)
XLA Ops:
  0.0 55.7 %hyena.1 = bf16[512,256]{1,0:T(8,128)(2,1)S(1)} custom-call(bf16[512,256]{1,0:T(8,128)(2,1)} %gate_h.1, bf16[512,256]{1,0:T(8,128)(2,1)} %key_h.1, bf16[512,256]{1,0:T(8,128)(2,1)} %value_h.1, f32[512,256]{1,0:T(8,128)} %filt_h.1, f32[1,256]{1,0:T(1,128)} %bitcast.1, bf16[256,8192]{1,0:T(8,128)(2,1)} %w_h.1, bf16[512,512]{1,0:T(8,128)(2,1)} %constant.4.clone.fwd_h, ...), custom_call_target="tpu_custom_call" | custom-call | tf_op jit(solution)/shard_map/hyena/pallas_call | solution.py:346
  55.7 0.7 %copy.10 = bf16[512,256]{1,0:T(8,128)(2,1)} copy(bf16[512,256]{1,0:T(8,128)(2,1)S(1)} %hyena.1) | data formatting | bytes 524288

commit v6 on v5

--- a/solution.py
+++ b/solution.py
@@ -298,7 +298,7 @@
             turn += [(step, r) for r in far + near]
         turns.append(turn)
     sums = {}
-    ahead = {6: (2, 6), 10: (1, 7), 13: (0,)}
+    ahead = {6: (2, 6), 10: (1, 7)}
     for n in range(len(turns[0])):
         if n == 0:
             hand_on(0)
@@ -327,6 +327,7 @@
                 r_rs.at[way, step, r],
                 (i, ((z + near) % RING) * 4 + q),
             )
+    partial(0, 0, POS)
     for r in (1, 3, 0, 2):
         rows = pl.ds(r * PIECE, PIECE)
         total = pbuf[ORDER.index(0), rows]

time: 57 us -> 57 us (level)
  no operation moved by 1% of the time
where the time goes in v6:
time: 57 us; the launch traced here: 56.4 us
  Pallas kernels  55.7 us (98%)
  local copies, waits for them, and re-layouts  0.71 us (1%)
    pallas_call x1, Pallas kernels, body(): pl.pallas_call(kernel, out_shape=pltpu.VMEM((POS, CHAN), BF16), in_specs=...  55.7 us

profile of v6, /device:TPU:1, one launch (start us, length us, event | category | flops | bytes accessed | tf_op | source)
XLA Modules:
  0.0 56.4 jit_solution(2511674607130999739)
XLA Ops:
  0.0 55.7 %hyena.1 = bf16[512,256]{1,0:T(8,128)(2,1)S(1)} custom-call(bf16[512,256]{1,0:T(8,128)(2,1)} %gate_h.1, bf16[512,256]{1,0:T(8,128)(2,1)} %key_h.1, bf16[512,256]{1,0:T(8,128)(2,1)} %value_h.1, f32[512,256]{1,0:T(8,128)} %filt_h.1, f32[1,256]{1,0:T(1,128)} %bitcast.1, bf16[256,8192]{1,0:T(8,128)(2,1)} %w_h.1, bf16[512,512]{1,0:T(8,128)(2,1)} %constant.4.clone.fwd_h, ...), custom_call_target="tpu_custom_call" | custom-call | tf_op jit(solution)/shard_map/hyena/pallas_call | solution.py:347
  55.7 0.7 %copy.10 = bf16[512,256]{1,0:T(8,128)(2,1)} copy(bf16[512,256]{1,0:T(8,128)(2,1)S(1)} %hyena.1) | data formatting | bytes 524288
